TPU v7x, 32 devices: a whole 2x2x4 slice. The times are simulated.
32 devices in a mesh: guide: 2 (over core), dp: 4 (over y, x), mp: 4 (over z).
Axes of the slice: x: 2, y: 2, z: 4, core: 2. Of those that a mesh axis runs over, the one named last changes fastest.
Arguments:
- states: bfloat16 [2, 32, 2048], P('guide', 'dp'), may hold values from -6 to 6
- lengths: int32 [2, 32], P('guide', 'dp'), may hold values from 1 to 32768, as said below
- sink_cache: bfloat16 [2, 32, 16, 2, 4, 128], P('guide', 'dp', 'mp'), may hold values from -48 to 48
- window_cache: bfloat16 [2, 32, 16, 2, 256, 128], P('guide', 'dp', 'mp'), may hold values from -360 to 360
- qkv_weight: bfloat16 [2048, 3, 16, 128], P(None, None, 'mp'), may hold values from -0.125 to 0.125
- out_weight: bfloat16 [16, 128, 2048], P('mp'), may hold values from -0.125 to 0.125
- expert_ids: int32 [2, 32, 8], replicated, may hold values from 0 to 63, all different within a row; in each aligned block of 8 rows (0 to 7, 8 to 15, ..., all dimensions but the last counted through in order) at most 2 rows name the same one
- route_weight: float32 [2, 32, 8], replicated, may hold values from 0.5 to 2
- expert_in: bfloat16 [2, 2048, 65536], P(None, None, ('guide', 'dp', 'mp')), may hold values from -0.125 to 0.125
- expert_out: bfloat16 [65536, 2048], P(('guide', 'dp', 'mp')), may hold values from -0.1875 to 0.1875
- vocab_weight: bfloat16 [2048, 26624], P(('guide', 'dp'), 'mp'), may hold values from -0.125 to 0.125
- guidance: float32 [32], P('dp'), may hold values from 1 to 5
Outputs:
- guided: float32 [32, 4, 2, 3328], P('dp', 'mp', 'guide')
Inputs may be any that keep to these rules, and one draw needn't show every extreme that they name: `lengths`: one stream of one request has exactly 32768 cached positions. `expert_ids`: taking the tokens streams first, then requests, in aligned blocks of 8 tokens (the tokens of one device), no expert is named by more than 2 tokens of a block, a bound that some block reaches.
All inputs are finite; a program needn't handle non-finite values.
Results may differ from a plain program's by a relative error of at most 0.025.
Values may be sent and summed in bfloat16 or wider, within the bound.
No kernel may reach another device: no remote copies, remote signals or barrier semaphores. Data moves between devices by JAX's collectives and lax.ppermute only.
A program may use at most 128 MiB of HBM per device.

v0:
```python
import math

import jax
import jax.numpy as jnp
from jax import lax
from jax.sharding import PartitionSpec as P

FFE = 1024


EPSILON = 1e-05


def partner(block, axis, stride):
    count = lax.axis_size(axis)
    route = []
    for low in range(count):
        high = low | 1 << stride
        if high != low and high < count:
            route += [(low, high), (high, low)]
    return lax.ppermute(block, axis, route)


def rms_norm(values):
    return values * lax.rsqrt(jnp.mean(values * values, axis=-1, keepdims=True) + EPSILON)


def rotate(vectors, positions):
    full_width = vectors.shape[-1]
    half_width = full_width // 2
    step_index = jnp.arange(half_width, dtype=jnp.float32)
    inverse = jnp.exp(step_index * (-2.0 * math.log(10000.0) / full_width))
    angles = positions.astype(jnp.float32)[:, None] * inverse[None, :]
    cosine = jnp.cos(angles)[:, None, :]
    sine_part = jnp.sin(angles)[:, None, :]
    first_half = vectors[..., :half_width]
    second = vectors[..., half_width:]
    return jnp.concatenate(
        [first_half * cosine - second * sine_part, second * cosine + first_half * sine_part],
        axis=-1,
    )


def body(
    states,
    lengths,
    sink_cache,
    window_cache,
    qkv_weight,
    out_weight,
    expert_ids,
    route_weight,
    expert_in,
    expert_out,
    vocab_weight,
    guidance,
):
    hidden = states[0]
    own_lengths = lengths[0]
    request_count = hidden.shape[0]
    normed = rms_norm(hidden.astype(jnp.float32)).astype(jnp.bfloat16)
    projected = jnp.einsum("rd,dthe->rthe", normed, qkv_weight, preferred_element_type=jnp.float32)
    query_rot = rotate(projected[:, 0], own_lengths).astype(jnp.bfloat16)
    fresh_key = rotate(projected[:, 1], own_lengths).astype(jnp.bfloat16)
    fresh_value = projected[:, 2].astype(jnp.bfloat16)
    sink_rows = sink_cache[0]
    window_rows = window_cache[0]
    sink_count = sink_rows.shape[3]
    window_count = window_rows.shape[3]
    root_size = math.sqrt(query_rot.shape[-1])
    sink_scores = (
        jnp.einsum(
            "rhe,rhse->rhs", query_rot, sink_rows[:, :, 0], preferred_element_type=jnp.float32
        )
        / root_size
    )
    window_scores = (
        jnp.einsum(
            "rhe,rhwe->rhw", query_rot, window_rows[:, :, 0], preferred_element_type=jnp.float32
        )
        / root_size
    )
    self_scores = (
        jnp.einsum("rhe,rhe->rh", query_rot, fresh_key, preferred_element_type=jnp.float32)
        / root_size
    )
    length_limit = own_lengths[:, None, None]
    sink_valid = jnp.arange(sink_count, dtype=jnp.int32)[None, None, :] < length_limit
    window_valid = (
        jnp.arange(window_count, dtype=jnp.int32)[None, None, :]
        >= sink_count + window_count - length_limit
    )
    sink_scores = jnp.where(sink_valid, sink_scores, -1e30)
    window_scores = jnp.where(window_valid, window_scores, -1e30)
    highest = jnp.maximum(
        jnp.maximum(jnp.max(sink_scores, axis=-1), jnp.max(window_scores, axis=-1)), self_scores
    )
    sink_exp = jnp.exp(sink_scores - highest[..., None])
    window_exp = jnp.exp(window_scores - highest[..., None])
    self_exp = jnp.exp(self_scores - highest)
    totals = jnp.sum(sink_exp, axis=-1) + jnp.sum(window_exp, axis=-1) + self_exp
    sink_prob = (sink_exp / totals[..., None]).astype(jnp.bfloat16)
    window_prob = (window_exp / totals[..., None]).astype(jnp.bfloat16)
    self_prob = (self_exp / totals).astype(jnp.bfloat16)
    mixture = (
        jnp.einsum(
            "rhs,rhse->rhe", sink_prob, sink_rows[:, :, 1], preferred_element_type=jnp.float32
        )
        + jnp.einsum(
            "rhw,rhwe->rhe", window_prob, window_rows[:, :, 1], preferred_element_type=jnp.float32
        )
        + self_prob[..., None].astype(jnp.float32) * fresh_value.astype(jnp.float32)
    ).astype(jnp.bfloat16)
    partial_out = jnp.einsum("rhe,hed->rd", mixture, out_weight, preferred_element_type=jnp.float32)
    attention_out = lax.psum(partial_out, "mp")
    residual = (hidden.astype(jnp.float32) + attention_out).astype(jnp.bfloat16)
    moe_in = rms_norm(residual.astype(jnp.float32)).astype(jnp.bfloat16)
    unit_count = expert_in.shape[2]
    unit_start = lax.axis_index(("guide", "dp", "mp")) * unit_count
    unit_expert = (unit_start + jnp.arange(unit_count, dtype=jnp.int32)) // FFE
    choice_rows = expert_ids.reshape(-1, expert_ids.shape[-1])
    route_rows = route_weight.reshape(-1, route_weight.shape[-1])
    coefficient = jnp.sum(
        jnp.where(
            choice_rows[:, :, None] == unit_expert[None, None, :], route_rows[:, :, None], 0.0
        ),
        axis=1,
    )
    piece = lax.all_gather(moe_in, ("guide", "dp"), axis=0, tiled=True)
    gate = jnp.dot(piece, expert_in[0], preferred_element_type=jnp.float32)
    upward = jnp.dot(piece, expert_in[1], preferred_element_type=jnp.float32)
    activated = (jax.nn.silu(gate) * upward * coefficient).astype(jnp.bfloat16)
    expert_terms = jnp.dot(activated, expert_out, preferred_element_type=jnp.float32)
    expert_part = lax.psum_scatter(expert_terms, ("guide", "dp"), scatter_dimension=0, tiled=True)
    expert_total = lax.psum(expert_part, "mp")
    final = rms_norm(residual.astype(jnp.float32) + expert_total).astype(jnp.bfloat16)
    final_all = lax.all_gather(final, ("guide", "dp"), axis=0, tiled=True)
    row_share = vocab_weight.shape[0]
    share_start = lax.axis_index(("guide", "dp")) * row_share
    final_cols = lax.dynamic_slice_in_dim(final_all, share_start, row_share, 1)
    logits = lax.psum_scatter(
        jnp.dot(final_cols, vocab_weight, preferred_element_type=jnp.float32).astype(jnp.bfloat16),
        ("guide", "dp"),
        scatter_dimension=0,
        tiled=True,
    ).astype(jnp.float32)
    half_width = logits.shape[1] // 2
    stream_index = lax.axis_index("guide")
    own_half = lax.dynamic_slice_in_dim(logits, stream_index * half_width, half_width, 1)
    other_half = lax.dynamic_slice_in_dim(logits, (1 - stream_index) * half_width, half_width, 1)
    partner_logits = partner(other_half, "guide", 0)
    is_conditional = stream_index == 0
    conditional = jnp.where(is_conditional, own_half, partner_logits)
    unconditional = jnp.where(is_conditional, partner_logits, own_half)
    guided = unconditional + guidance[:, None] * (conditional - unconditional)
    return guided.reshape(request_count, 1, 1, half_width)


def solution(mesh):
    in_specs = (
        P("guide", "dp", None),
        P("guide", "dp"),
        P("guide", "dp", "mp", None, None, None),
        P("guide", "dp", "mp", None, None, None),
        P(None, None, "mp", None),
        P("mp", None, None),
        P(),
        P(),
        P(None, None, ("guide", "dp", "mp")),
        P(("guide", "dp", "mp"), None),
        P(("guide", "dp"), "mp"),
        P("dp"),
    )
    out_specs = P("dp", "mp", "guide", None)
    return jax.shard_map(body, mesh=mesh, in_specs=in_specs, out_specs=out_specs, check_vma=False)
```

profile of v0, /device:TPU:0, one launch (start us, length us, event | category | flops | bytes accessed | tf_op | source)
XLA Modules:
  0.0 245.4 jit_solution(16714871325069011965)
XLA Ops:
  6.5 0.0 copy-start
  6.5 0.0 all-reduce.3.cloned.1.call-start
  6.5 0.0 copy-start.2
  6.6 0.8 bitcast_convert_fusion
  7.4 1.0 broadcast_subtract_fusion
  8.3 1.0 fusion.30
  9.4 0.0 copy-start.9
  9.4 3.8 %fusion.6 = f32[8,3,4,128]{3,0,2,1:T(8,128)S(1)} fusion(bf16[2048,3,4,128]{3,2,1,0:T(4,128)(2,1)} %param.16, bf16[1,8,2048]{2,1,0:T(8,128)(2,1)} %param.12, f32[8]{0:T(128)S(1)} %add_rsqrt_fusion.2), kind=kOutput, calls=%fused_computation.7 | convolution fusion | flops 50380800 | bytes 6373408 | tf_op jit(solution)/shard_map/rd,dthe->rthe/dot_general | solution.py:62
  13.2 0.1 iota_compare_fusion
  13.3 0.1 multiply_cosine_fusion
  13.4 0.7 subtract_convert_fusion
  14.1 0.1 fusion.61
  14.1 0.0 copy-done.2
  14.1 0.6 fusion.18
  14.8 0.0 copy-done.8
  14.8 0.8 fusion.40
  15.6 0.8 copy.37
  16.4 0.0 copy-done.9
  16.4 0.9 fusion.46
  17.3 0.1 fusion.43
  17.4 0.2 fusion.42
  17.6 0.0 copy-start.5
  17.6 0.7 fusion.47
  18.3 0.1 copy.42
  18.4 0.9 fusion.41
  19.4 2.0 fusion.17
  21.4 2.7 %convolution_bitcast_fusion = f32[8,2048]{1,0:T(8,128)} fusion(bf16[4,128,2048]{2,1,0:T(8,128)(2,1)} %param.17, f32[8,4,1,128]{3,2,1,0:T(1,128)S(1)} %fusion.17, f32[8,4,1,128]{3,2,1,0:T(1,128)S(1)} %fusion.41, f32[8,3,4,128]{3,0,2,1:T(8,128)S(1)} %fusion.6, f32[8,4]{0,1:T(4,128)S(1)} %get-tuple-element.7), kind=kOutput, calls=%fused_computation.13 | convolution fusion | flops 16797696 | bytes 2205696 | tf_op jit(solution)/shard_map/rhe,hed->rd/dot_general | solution.py:114
  24.0 0.0 all-reduce.3.cloned.1.call-update
  24.0 0.0 reduce-scatter.3.cloned.1.call-start
  24.1 0.0 copy-done.5
  24.1 0.1 copy.47
  24.2 0.0 copy-done.6
  24.2 0.1 copy.48
  24.3 2.1 select_reduce_fusion
  26.4 34.5 %all-reduce.3.cloned.1.call-done = f32[8,2048]{1,0:T(8,128)} async-done(((f32[8,2048]{1,0:T(8,128)}), f32[8,2048]{1,0:T(8,128)}) %all-reduce.3.cloned.1.call-update) | async-done | bytes 65552 | tf_op jit(solution)/shard_map/psum | solution.py:115
  60.9 0.0 copy-done.4
  60.9 1.0 fusion.28
  61.9 0.1 fusion.29
  61.9 23.9 %all_gather.6 = bf16[64,2048]{1,0:T(8,128)(2,1)S(1)} all-gather(bf16[8,2048]{1,0:T(8,128)(2,1)S(1)} %fusion.29), channel_id=1, replica_groups=mesh['guide'=2,'dp'=4,'mp'=4] {'guide','dp'}, dimensions={0}, use_global_device_ids=true | all-gather | bytes 294912 | tf_op jit(solution)/shard_map/all_gather | solution.py:129
  85.8 0.7 copy-done.1
  86.5 5.8 %fusion.2 = f32[64,2048]{1,0:T(8,128)} fusion(bf16[64,2048]{1,0:T(8,128)(2,1)S(1)} %all_gather.6, bf16[2,2048,2048]{2,1,0:T(8,128)(2,1)} %param.20), kind=kOutput, calls=%fused_computation.2 | convolution fusion | flops 536870912 | bytes 9175040 | tf_op jit(solution)/shard_map/dot_general | solution.py:130
  92.3 10.0 %fusion.20 = f32[64,2048]{1,0:T(8,128)} fusion(bf16[2048,2048]{1,0:T(8,128)(2,1)} %param.21, f32[64,2048]{1,0:T(8,128)} %select_reduce_fusion, bf16[64,2048]{1,0:T(8,128)(2,1)} %copy-done.1, bf16[2,2048,2048]{2,1,0:T(8,128)(2,1)} %param.20, f32[64,2048]{1,0:T(8,128)} %fusion.2), kind=kOutput, calls=%fused_computation.18 | convolution fusion | flops 1074659328 | bytes 18612224 | tf_op jit(solution)/shard_map/dot_general | solution.py:133
  102.3 0.0 reduce-scatter.3.cloned.1.call-update
  102.3 0.0 all-reduce.5.cloned.1.call-start
  102.4 33.0 %reduce-scatter.3.cloned.1.call-done = f32[8,2048]{1,0:T(8,128)} async-done(((f32[64,2048]{1,0:T(8,128)}), f32[8,2048]{1,0:T(8,128)}) %reduce-scatter.3.cloned.1.call-update) | async-done | bytes 65552 | tf_op jit(solution)/shard_map/reduce_scatter | solution.py:134
  135.4 0.0 all-reduce.5.cloned.1.call-update
  135.4 0.0 reduce-scatter.5.cloned.1.call-start
  135.5 36.3 %all-reduce.5.cloned.1.call-done = f32[8,2048]{1,0:T(8,128)} async-done(((f32[8,2048]{1,0:T(8,128)}), f32[8,2048]{1,0:T(8,128)}) %all-reduce.5.cloned.1.call-update) | async-done | bytes 65552 | tf_op jit(solution)/shard_map/psum | solution.py:135
  171.8 1.0 multiply_reduce_fusion
  172.7 0.9 multiply_convert_fusion
  173.7 23.9 %all_gather.7 = bf16[64,2048]{1,0:T(8,128)(2,1)S(1)} all-gather(bf16[8,2048]{1,0:T(8,128)(2,1)S(1)} %multiply_convert_fusion), channel_id=1, replica_groups=mesh['guide'=2,'dp'=4,'mp'=4] {'guide','dp'}, dimensions={0}, use_global_device_ids=true | all-gather | bytes 294912 | tf_op jit(solution)/shard_map/all_gather | solution.py:137
  197.5 0.0 copy-done
  197.5 1.6 convolution_convert_fusion
  199.1 0.0 reduce-scatter.5.cloned.1.call-update
  199.2 34.2 %reduce-scatter.5.cloned.1.call-done = bf16[8,6656]{1,0:T(8,128)(2,1)} async-done(((bf16[64,6656]{1,0:T(8,128)(2,1)}), bf16[8,6656]{1,0:T(8,128)(2,1)}) %reduce-scatter.5.cloned.1.call-update) | async-done | bytes 106512 | tf_op jit(solution)/shard_map/reduce_scatter | solution.py:141
  233.4 0.9 convert_element_type.83
  234.3 0.0 copy-start.3
  234.3 0.7 copy-done.3
  235.0 0.7 constant_dynamic-slice_fusion
  235.6 0.0 collective-permute-start
  235.6 1.5 collective-permute-done
  237.1 0.0 copy-done.7
  237.1 1.0 add_bitcast_fusion
  238.1 0.8 copy.34
  (17 shorter events, 0.1 us)
Async XLA Ops:
  6.5 191.0 %copy-start = (bf16[256,6656]{1,0:T(8,128)(2,1)S(1)}, bf16[256,6656]{1,0:T(8,128)(2,1)}, u32[]{:S(2)}) copy-start(bf16[256,6656]{1,0:T(8,128)(2,1)} %param.22) | copy-start | bytes 10223620
  6.5 54.3 %all-reduce.3.cloned.1.call-start = ((), (), s32[]{:S(2)}) async-start(), calls=%async_computation.2 | async-start | bytes 131072 | tf_op jit(solution)/shard_map/psum | solution.py:115
  6.5 7.6 %copy-start.2 = (bf16[1,8,4,2,256,128]{5,4,3,2,1,0:T(8,128)(2,1)S(1)}, bf16[1,8,4,2,256,128]{5,4,3,2,1,0:T(8,128)(2,1)}, u32[]{:S(2)}) copy-start(bf16[1,8,4,2,256,128]{5,4,3,2,1,0:T(8,128)(2,1)} %param.15) | copy-start | bytes 12582916
  9.4 5.4 %copy-start.8 = (bf16[1,8,4,2,4,128]{5,4,3,2,1,0:T(4,128)(2,1)S(1)}, bf16[1,8,4,2,4,128]{5,4,3,2,1,0:T(4,128)(2,1)}, u32[]{:S(2)}) copy-start(bf16[1,8,4,2,4,128]{5,4,3,2,1,0:T(4,128)(2,1)} %param.14) | copy-start | bytes 196612
  9.4 7.0 %copy-start.9 = (s32[1,8]{1,0:T(1,128)S(1)}, s32[1,8]{1,0:T(1,128)}, u32[]{:S(2)}) copy-start(s32[1,8]{1,0:T(1,128)} %param.13) | copy-start | bytes 100
  13.2 47.7 %copy-start.4 = (bf16[1,8,2048]{2,1,0:T(8,128)(2,1)S(1)}, bf16[1,8,2048]{2,1,0:T(8,128)(2,1)}, u32[]{:S(2)}) copy-start(bf16[1,8,2048]{2,1,0:T(8,128)(2,1)} %param.12) | copy-start | bytes 98308
  17.6 6.5 %copy-start.5 = (s32[2,32,8]{1,2,0:T(8,128)S(1)}, s32[2,32,8]{1,2,0:T(8,128)}, u32[]{:S(2)}) copy-start(s32[2,32,8]{1,2,0:T(8,128)} %param.18) | copy-start | bytes 6148
  18.3 5.9 %copy-start.6 = (f32[2,32,8]{1,2,0:T(8,128)S(1)}, f32[2,32,8]{1,2,0:T(8,128)}, u32[]{:S(2)}) copy-start(f32[2,32,8]{1,2,0:T(8,128)} %param.19) | copy-start | bytes 6148
  24.0 111.4 %reduce-scatter.3.cloned.1.call-start = ((), (), s32[]{:S(2)}) async-start(), calls=%async_computation.3 | async-start | bytes 589824 | tf_op jit(solution)/shard_map/reduce_scatter | solution.py:134
  85.8 0.7 copy-start.1
  102.3 134.8 %copy-start.7 = (f32[8]{0:T(128)S(1)}, f32[8]{0:T(128)}, u32[]{:S(2)}) copy-start(f32[8]{0:T(128)} %param.23) | copy-start | bytes 100
  102.3 69.4 %all-reduce.5.cloned.1.call-start = ((), (), s32[]{:S(2)}) async-start(), calls=%async_computation.4 | async-start | bytes 131072 | tf_op jit(solution)/shard_map/psum | solution.py:135
  135.4 97.9 %reduce-scatter.5.cloned.1.call-start = ((), (), s32[]{:S(2)}) async-start(), calls=%async_computation.5 | async-start | bytes 958464 | tf_op jit(solution)/shard_map/reduce_scatter | solution.py:141
  234.3 0.7 copy-start.3
  235.6 1.5 collective-permute-start
Sparse Core Ops, SparseCore 0:
  24.2 36.6 all-reduce.2
  102.4 32.9 reduce-scatter.2
  137.7 33.9 all-reduce.4
  199.3 34.0 reduce-scatter.4
where the time goes:
time: 246 us; the launch traced here: 245 us
  waiting for transfers between devices  140 us (57%)
  blocking collectives  47.7 us (19%)
  matrix products  28.2 us (11%)
  between operations  13.3 us (5%)
  other arithmetic  12.7 us (5%)
  local copies, waits for them, and re-layouts  3.89 us (2%)
    psum x1, waiting for transfers between devices, body(): expert_total = lax.psum(expert_part, 'mp')  36.3 us
    psum x1, waiting for transfers between devices, body(): attention_out = lax.psum(partial_out, 'mp')  34.5 us
    reduce_scatter x1, waiting for transfers between devices, body(): lax.psum_scatter(jnp.dot(final_cols, vocab_weight, preferred_element_type...  34.2 us
    reduce_scatter x1, waiting for transfers between devices, body(): lax.psum_scatter(expert_terms, ('guide', 'dp'), scatter_dimension=0, tile...  33 us
    all_gather x1, blocking collectives, body(): piece = lax.all_gather(moe_in, ('guide', 'dp'), axis=0, tiled=True)  23.9 us
    all_gather x1, blocking collectives, body(): final_all = lax.all_gather(final, ('guide', 'dp'), axis=0, tiled=True)  23.9 us
    dot_general x1, matrix products, body(): jnp.dot(activated, expert_out, preferred_element_type=jnp.float32)  10 us
    dot_general x1, matrix products, body(): gate = jnp.dot(piece, expert_in[0], preferred_element_type=jnp.float32)  5.77 us
  transfers between devices with their start and end apart: 5, of which 5 were waited for; matrix products, arithmetic and copies ran while one was open for 1% of the time, Pallas kernels for 0%

commit v1 on v0

v1 whole, which is shorter than its diff:
```python
import math

import jax
import jax.numpy as jnp
from jax import lax
from jax.sharding import PartitionSpec as P

FFE = 1024

EPSILON = 1e-05

ROWS = ("guide", "dp")
DIRECT = 8


def swap(blocks, axis):
    count = lax.axis_size(axis)
    if count <= DIRECT:
        return [blocks[0]] + [
            lax.ppermute(blocks[j], axis, [(i, i ^ j) for i in range(count)]) for j in range(1, count)
        ]
    order = lax.axis_index(axis) ^ jnp.arange(count, dtype=jnp.int32)
    sent = jnp.take(jnp.stack(blocks), order, axis=0)
    received = lax.all_to_all(sent, axis, 0, 0, tiled=True)
    return list(jnp.take(received, order, axis=0))


def spread(block, axis):
    return swap([block] * lax.axis_size(axis), axis)


def rotate(vectors, positions):
    full_width = vectors.shape[-1]
    half_width = full_width // 2
    step_index = jnp.arange(half_width, dtype=jnp.float32)
    inverse = jnp.exp(step_index * (-2.0 * math.log(10000.0) / full_width))
    angles = positions.astype(jnp.float32)[:, None] * inverse[None, :]
    cosine = jnp.cos(angles)[:, None, :]
    sine_part = jnp.sin(angles)[:, None, :]
    first_half = vectors[..., :half_width]
    second = vectors[..., half_width:]
    return jnp.concatenate(
        [first_half * cosine - second * sine_part, second * cosine + first_half * sine_part],
        axis=-1,
    )


def rms_norm(values):
    return values * lax.rsqrt(jnp.mean(values * values, axis=-1, keepdims=True) + EPSILON)


def attend(hidden, own_lengths, sink_rows, window_rows, qkv_weight, out_weight):
    normed = rms_norm(hidden.astype(jnp.float32)).astype(jnp.bfloat16)
    projected = jnp.einsum("rd,dthe->rthe", normed, qkv_weight, preferred_element_type=jnp.float32)
    query_rot = rotate(projected[:, 0], own_lengths).astype(jnp.bfloat16)
    fresh_key = rotate(projected[:, 1], own_lengths).astype(jnp.bfloat16)
    fresh_value = projected[:, 2].astype(jnp.bfloat16)
    sink_count = sink_rows.shape[3]
    window_count = window_rows.shape[3]
    root_size = math.sqrt(query_rot.shape[-1])
    sink_scores = (
        jnp.einsum(
            "rhe,rhse->rhs", query_rot, sink_rows[:, :, 0], preferred_element_type=jnp.float32
        )
        / root_size
    )
    window_scores = (
        jnp.einsum(
            "rhe,rhwe->rhw", query_rot, window_rows[:, :, 0], preferred_element_type=jnp.float32
        )
        / root_size
    )
    self_scores = (
        jnp.einsum("rhe,rhe->rh", query_rot, fresh_key, preferred_element_type=jnp.float32)
        / root_size
    )
    length_limit = own_lengths[:, None, None]
    sink_valid = jnp.arange(sink_count, dtype=jnp.int32)[None, None, :] < length_limit
    window_valid = (
        jnp.arange(window_count, dtype=jnp.int32)[None, None, :]
        >= sink_count + window_count - length_limit
    )
    sink_scores = jnp.where(sink_valid, sink_scores, -1e30)
    window_scores = jnp.where(window_valid, window_scores, -1e30)
    highest = jnp.maximum(
        jnp.maximum(jnp.max(sink_scores, axis=-1), jnp.max(window_scores, axis=-1)), self_scores
    )
    sink_exp = jnp.exp(sink_scores - highest[..., None])
    window_exp = jnp.exp(window_scores - highest[..., None])
    self_exp = jnp.exp(self_scores - highest)
    totals = jnp.sum(sink_exp, axis=-1) + jnp.sum(window_exp, axis=-1) + self_exp
    sink_prob = (sink_exp / totals[..., None]).astype(jnp.bfloat16)
    window_prob = (window_exp / totals[..., None]).astype(jnp.bfloat16)
    self_prob = (self_exp / totals).astype(jnp.bfloat16)
    mixture = (
        jnp.einsum(
            "rhs,rhse->rhe", sink_prob, sink_rows[:, :, 1], preferred_element_type=jnp.float32
        )
        + jnp.einsum(
            "rhw,rhwe->rhe", window_prob, window_rows[:, :, 1], preferred_element_type=jnp.float32
        )
        + self_prob[..., None].astype(jnp.float32) * fresh_value.astype(jnp.float32)
    ).astype(jnp.bfloat16)
    return jnp.einsum("rhe,hed->rd", mixture, out_weight, preferred_element_type=jnp.float32)


def body(
    states,
    lengths,
    sink_cache,
    window_cache,
    qkv_weight,
    out_weight,
    expert_ids,
    route_weight,
    expert_in,
    expert_out,
    vocab_weight,
    guidance,
):
    hidden = states[0]
    request_count, width = hidden.shape
    group = lax.axis_size(ROWS)
    place = lax.axis_index(ROWS)
    streams_apart = group // lax.axis_size("guide")
    stream_index = lax.axis_index("guide")
    order = place ^ jnp.arange(group, dtype=jnp.int32)

    partial_out = attend(hidden, lengths[0], sink_cache[0], window_cache[0], qkv_weight, out_weight)
    partials = spread(partial_out.astype(jnp.bfloat16), "mp")
    attention_out = sum(block.astype(jnp.float32) for block in partials)
    own_residual = (hidden.astype(jnp.float32) + attention_out).astype(jnp.bfloat16)

    residual = jnp.concatenate(spread(own_residual, ROWS), axis=0)
    moe_in = rms_norm(residual.astype(jnp.float32)).astype(jnp.bfloat16)

    unit_count = expert_in.shape[2]
    unit_start = lax.axis_index(("guide", "dp", "mp")) * unit_count
    unit_expert = (unit_start + jnp.arange(unit_count, dtype=jnp.int32)) // FFE
    top = expert_ids.shape[-1]
    choice_rows = jnp.take(expert_ids.reshape(group, request_count, top), order, axis=0).reshape(-1, top)
    route_rows = jnp.take(route_weight.reshape(group, request_count, top), order, axis=0).reshape(-1, top)
    coefficient = jnp.sum(
        jnp.where(
            choice_rows[:, :, None] == unit_expert[None, None, :], route_rows[:, :, None], 0.0
        ),
        axis=1,
    )
    gate = jnp.dot(moe_in, expert_in[0], preferred_element_type=jnp.float32)
    upward = jnp.dot(moe_in, expert_in[1], preferred_element_type=jnp.float32)
    activated = (jax.nn.silu(gate) * upward * coefficient).astype(jnp.bfloat16)
    expert_terms = jnp.dot(activated, expert_out, preferred_element_type=jnp.float32).astype(jnp.bfloat16)

    share = vocab_weight.shape[0]
    sent = []
    for j in range(group):
        columns = lax.dynamic_slice_in_dim(expert_terms, (place ^ j) * share, share, 1)
        rows = columns.reshape(group, request_count, share)
        sent.append(jnp.concatenate([rows[i ^ j] for i in range(group)], axis=0))
    expert_part = sum(block.astype(jnp.float32) for block in swap(sent, ROWS))
    expert_total = sum(
        block.astype(jnp.float32) for block in spread(expert_part.astype(jnp.bfloat16), "mp")
    )
    own_columns = lax.dynamic_slice_in_dim(residual, place * share, share, 1)
    summed = own_columns.astype(jnp.float32) + expert_total

    squares = jnp.sum(summed * summed, axis=-1).reshape(group, request_count)
    note = jnp.concatenate([squares, guidance[None, :]], axis=0)
    notes = spread(note, ROWS)
    square_total = jnp.stack(
        [sum(notes[j][i ^ j] for j in range(group)) for i in range(group)]
    ).reshape(-1, 1)
    scale = lax.rsqrt(square_total / width + EPSILON)
    weight = jnp.stack([notes[i][group] for i in range(streams_apart)]).reshape(-1, 1)
    is_conditional = stream_index == 0
    own_factor = jnp.where(is_conditional, weight, 1.0 - weight)

    raw = jnp.dot(summed.astype(jnp.bfloat16), vocab_weight, preferred_element_type=jnp.float32)
    cut = streams_apart * request_count
    mixed = raw[:cut] * (scale[:cut] * own_factor) + raw[cut:] * (scale[cut:] * (1.0 - own_factor))
    half_width = mixed.shape[1] // 2
    mixed = mixed.astype(jnp.bfloat16).reshape(streams_apart, request_count, 2 * half_width)
    sent = [
        lax.dynamic_slice_in_dim(
            mixed[j % streams_apart], (stream_index ^ (j // streams_apart)) * half_width, half_width, 1
        )
        for j in range(group)
    ]
    guided = sum(block.astype(jnp.float32) for block in swap(sent, ROWS))
    return guided.reshape(request_count, 1, 1, half_width)


def solution(mesh):
    in_specs = (
        P("guide", "dp", None),
        P("guide", "dp"),
        P("guide", "dp", "mp", None, None, None),
        P("guide", "dp", "mp", None, None, None),
        P(None, None, "mp", None),
        P("mp", None, None),
        P(),
        P(),
        P(None, None, ("guide", "dp", "mp")),
        P(("guide", "dp", "mp"), None),
        P(("guide", "dp"), "mp"),
        P("dp"),
    )
    out_specs = P("dp", "mp", "guide", None)
    return jax.shard_map(body, mesh=mesh, in_specs=in_specs, out_specs=out_specs, check_vma=False)
```

time: 246 us -> 124 us (0.50)
  waiting for transfers between devices: 140 us -> 12.7 us
  blocking collectives: 47.7 us -> 0 us
  starting transfers between devices: 0.13 us -> 37.6 us
  local copies, waits for them, and re-layouts: 3.89 us -> 22.4 us
  between operations: 13.3 us -> 0.33 us
  other arithmetic: 12.7 us -> 20.9 us
    psum x2 -> x0, waiting for transfers between devices: 70.7 us -> none  [the longest x1 36.3 us: body(): expert_total = lax.psum(expert_part, 'mp')]
    reduce_scatter x2 -> x0, waiting for transfers between devices: 67.2 us -> none  [the longest x1 34.2 us: body(): lax.psum_scatter(jnp.dot(final_cols, vocab_weight, preferred_element_type...]
    all_gather x2 -> x0, blocking collectives: 47.7 us -> none  [the longest x1 23.9 us: body(): piece = lax.all_gather(moe_in, ('guide', 'dp'), axis=0, tiled=True)]
    ppermute x1 -> x34, starting transfers between devices: 0.01 us -> 37.6 us  [swap(): lax.ppermute(blocks[j], axis, [(i, i ^ j) for i in range(count)])]
    unnamed x20 -> x41, local copies, waits for them, and re-layouts: 1.4 us -> 12.8 us
    ppermute x1 -> x34, waiting for transfers between devices: 1.52 us -> 12.7 us  [swap(): lax.ppermute(blocks[j], axis, [(i, i ^ j) for i in range(count)])]
    add x0 -> x4, other arithmetic: none -> 3.47 us  [body(): sum((notes[j][i ^ j] for j in range(group)))]
    concatenate x0 -> x3, local copies, waits for them, and re-layouts: none -> 3.22 us  [the longest x2 2.6 us: body(): sent.append(jnp.concatenate([rows[i ^ j] for i in range(group)], axis=0))]
  transfers between devices with their start and end apart: 5 -> 34, of which waited for: 5 -> 11; matrix products, arithmetic and copies ran while one was open for 1% -> 21% of each run, Pallas kernels for 0% -> 0%
where the time goes in v1:
time: 124 us; the launch traced here: 123 us
  starting transfers between devices  37.6 us (30%)
  matrix products  28.7 us (23%)
  local copies, waits for them, and re-layouts  22.4 us (18%)
  other arithmetic  20.9 us (17%)
  waiting for transfers between devices  12.7 us (10%)
    ppermute x34, starting transfers between devices, swap(): lax.ppermute(blocks[j], axis, [(i, i ^ j) for i in range(count)])  37.6 us
    unnamed x41, local copies, waits for them, and re-layouts  12.8 us
    ppermute x34, waiting for transfers between devices, swap(): lax.ppermute(blocks[j], axis, [(i, i ^ j) for i in range(count)])  12.7 us
    dot_general x1, matrix products, body(): jnp.dot(activated, expert_out, preferred_element_type=jnp.float32)  10 us
    dot_general x1, matrix products, body(): gate = jnp.dot(moe_in, expert_in[0], preferred_element_type=jnp.float32)  5.95 us
    dot_general x1, matrix products, attend(): jnp.einsum('rd,dthe->rthe', normed, qkv_weight, preferred_element_type=jn...  3.79 us
    add x4, other arithmetic, body(): sum((notes[j][i ^ j] for j in range(group)))  3.47 us
    dot_general x1, matrix products, body(): jnp.dot(summed.astype(jnp.bfloat16), vocab_weight, preferred_element_type...  2.66 us
  transfers between devices with their start and end apart: 34, of which 11 were waited for; matrix products, arithmetic and copies ran while one was open for 21% of the time, Pallas kernels for 0%

profile of v1, /device:TPU:0, one launch (start us, length us, event | category | flops | bytes accessed | tf_op | source)
XLA Modules:
  0.0 122.7 jit_solution(9248940510214501154)
XLA Ops:
  0.0 0.8 bitcast_convert_fusion
  0.8 1.0 broadcast_subtract_fusion
  1.8 1.0 fusion.35
  2.8 3.8 %fusion.6 = f32[8,3,4,128]{3,0,2,1:T(8,128)S(1)} fusion(bf16[2048,3,4,128]{3,2,1,0:T(4,128)(2,1)} %param.16, bf16[1,8,2048]{2,1,0:T(8,128)(2,1)} %param.12, f32[8]{0:T(128)S(1)} %add_rsqrt_fusion.2), kind=kOutput, calls=%fused_computation.8 | convolution fusion | flops 50380800 | bytes 6373408 | tf_op jit(solution)/shard_map/rd,dthe->rthe/dot_general | solution.py:54
  9.0 0.8 copy.47
  9.8 0.9 fusion.52
  11.9 0.9 fusion.47
  12.8 2.0 %fusion.18 = f32[8,4,1,128]{3,2,1,0:T(1,128)S(1)} fusion(bf16[8,4,2,256,128]{4,3,2,1,0:T(8,128)(2,1)} %bitcast.132, bf16[8,4,256,1]{2,0,1,3:T(8,128)(2,1)} %fusion.53), kind=kOutput, calls=%fused_computation.18 | convolution fusion | flops 2097152 | bytes 2129920 | tf_op jit(solution)/shard_map/rhw,rhwe->rhe/dot_general | solution.py:99
  14.8 2.0 %fusion.17 = bf16[8,2048]{1,0:T(8,128)(2,1)S(1)} fusion(bf16[4,128,2048]{2,1,0:T(8,128)(2,1)} %param.17, f32[8,4,1,128]{3,2,1,0:T(1,128)S(1)} %fusion.18, f32[8,4,1,128]{3,2,1,0:T(1,128)S(1)} %fusion.47, f32[8,3,4,128]{3,0,2,1:T(8,128)S(1)} %fusion.6, f32[8,4]{0,1:T(4,128)S(1)} %get-tuple-element.7), kind=kOutput, calls=%fused_computation.16 | convolution fusion | flops 16814080 | bytes 2172928 | tf_op jit(solution)/shard_map/rhe,hed->rd/dot_general | solution.py:104
  16.8 3.0 %collective-permute-start = (bf16[8,2048]{1,0:T(8,128)(2,1)S(1)}, bf16[8,2048]{1,0:T(8,128)(2,1)}, u32[]{:S(2)}, u32[]{:S(2)}) collective-permute-start(bf16[8,2048]{1,0:T(8,128)(2,1)S(1)} %fusion.17), channel_id=1, source_target_pairs={{0,1},{1,0},{2,3},{3,2},{4,5},{5,4},{6,7},{7,6},{8,9},{9,8},{10,11... | collective-permute-start | bytes 98312 | tf_op jit(solution)/shard_map/ppermute | solution.py:20
  19.9 2.6 %collective-permute-start.1 = (bf16[8,2048]{1,0:T(8,128)(2,1)S(1)}, bf16[8,2048]{1,0:T(8,128)(2,1)}, u32[]{:S(2)}, u32[]{:S(2)}) collective-permute-start(bf16[8,2048]{1,0:T(8,128)(2,1)S(1)} %fusion.17), channel_id=1, source_target_pairs={{0,2},{1,3},{2,0},{3,1},{4,6},{5,7},{6,4},{7,5},{8,10},{9,11},{10,... | collective-permute-start | bytes 98312 | tf_op jit(solution)/shard_map/ppermute | solution.py:20
  22.8 1.2 gather_fusion
  24.0 1.2 gather_fusion.1
  25.2 0.8 bitcast_select_fusion.1
  26.0 0.8 bitcast_select_fusion
  26.9 1.4 %collective-permute-done.2 = bf16[8,2048]{1,0:T(8,128)(2,1)} collective-permute-done((bf16[8,2048]{1,0:T(8,128)(2,1)S(1)}, bf16[8,2048]{1,0:T(8,128)(2,1)}, u32[]{:S(2)}, u32[]{:S(2)}) %collective-permute-start.2) | collective-permute-done | bytes 32800 | tf_op jit(solution)/shard_map/ppermute | solution.py:20
  28.3 1.4 %constant_dynamic-update-slice_fusion.7 = (bf16[64,2048]{1,0:T(8,128)(2,1)}, bf16[8,2048]{1,0:T(8,128)(2,1)}) fusion(bf16[8,2048]{1,0:T(8,128)(2,1)} %collective-permute-done.2, bf16[8,2048]{1,0:T(8,128)(2,1)} %collective-permute-done.1, bf16[8,2048]{1,0:T(8,128)(2,1)} %collective-permute-done, bf16[8,2048]{1,0:T(8,128)(2,1)S(1)} %fusion.17, ...), kind=kLoop, calls=%fused_computation.46 | loop fusion | flops 163839 | bytes 229376
  29.7 1.5 %collective-permute-start.3 = (bf16[8,2048]{1,0:T(8,128)(2,1)}, bf16[8,2048]{1,0:T(8,128)(2,1)S(1)}, u32[]{:S(2)}, u32[]{:S(2)}) collective-permute-start(bf16[8,2048]{1,0:T(8,128)(2,1)} %get-tuple-element.6), channel_id=1, source_target_pairs={{0,4},{4,0},{8,12},{12,8},{16,20},{20,16},{24,28},{28,24},{1,5},{5... | collective-permute-start | bytes 98312 | tf_op jit(solution)/shard_map/ppermute | solution.py:20
  31.2 2.1 %select_reduce_fusion = f32[64,2048]{1,0:T(8,128)} fusion(f32[64,8]{1,0:T(8,128)S(1)} %bitcast_select_fusion, s32[2048]{0:T(1024)S(1)} %add_select_fusion, s32[64,8]{1,0:T(8,128)S(1)} %bitcast_select_fusion.1), kind=kLoop, calls=%fused_computation.10 | loop fusion | flops 3014656 | bytes 536576 | tf_op jit(solution)/shard_map/reduce_sum | solution.py:143
  33.3 1.5 %collective-permute-start.4 = (bf16[8,2048]{1,0:T(8,128)(2,1)}, bf16[8,2048]{1,0:T(8,128)(2,1)S(1)}, u32[]{:S(2)}, u32[]{:S(2)}) collective-permute-start(bf16[8,2048]{1,0:T(8,128)(2,1)} %get-tuple-element.6), channel_id=1, source_target_pairs={{0,8},{4,12},{8,0},{12,4},{16,24},{20,28},{24,16},{28,20},{1,9},{5... | collective-permute-start | bytes 98312 | tf_op jit(solution)/shard_map/ppermute | solution.py:20
  35.3 1.6 %collective-permute-start.7 = (bf16[8,2048]{1,0:T(8,128)(2,1)}, bf16[8,2048]{1,0:T(8,128)(2,1)S(1)}, u32[]{:S(2)}, u32[]{:S(2)}) collective-permute-start(bf16[8,2048]{1,0:T(8,128)(2,1)} %get-tuple-element.6), channel_id=1, source_target_pairs={{0,20},{4,16},{8,28},{12,24},{16,4},{20,0},{24,12},{28,8},{1,21},{... | collective-permute-start | bytes 98312 | tf_op jit(solution)/shard_map/ppermute | solution.py:20
  37.0 1.1 collective-permute-start.8
  43.8 1.1 fusion.24
  44.9 5.9 %fusion.2 = f32[64,2048]{1,0:T(8,128)} fusion(bf16[2,2048,2048]{2,1,0:T(8,128)(2,1)} %param.20, bf16[64,2048]{1,0:T(8,128)(2,1)} %constant_dynamic-update-slice_fusion, f32[64]{0:T(128)S(1)} %add_rsqrt_fusion.1), kind=kOutput, calls=%fused_computation.4 | convolution fusion | flops 537264128 | bytes 9175296 | tf_op jit(solution)/shard_map/dot_general | solution.py:149
  50.8 10.0 %convolution_convert_fusion = bf16[64,2048]{1,0:T(8,128)(2,1)} fusion(bf16[2048,2048]{1,0:T(8,128)(2,1)} %param.21, f32[64,2048]{1,0:T(8,128)} %select_reduce_fusion, bf16[2,2048,2048]{2,1,0:T(8,128)(2,1)} %param.20, f32[64,2048]{1,0:T(8,128)} %fusion.2, bf16[64,2048]{1,0:T(8,128)(2,1)} %constant_dynamic-update-slice_fusion, f32[64]{0:T(128)S(1)} %add_rsqrt_fusion.1), kind=kOutput, calls=%fused_computation.14 | convolution fusion | flops 1075183616 | bytes 18350336 | tf_op jit(solution)/shard_map/dot_general | solution.py:152
  60.8 0.8 fusion.73
  61.7 0.8 collective-permute-start.11
  63.8 1.4 %collective-permute-start.15 = (bf16[64,256]{1,0:T(8,128)(2,1)}, bf16[64,256]{1,0:T(8,128)(2,1)S(1)}, u32[]{:S(2)}, u32[]{:S(2)}) collective-permute-start(bf16[64,256]{1,0:T(8,128)(2,1)} %pad_maximum_fusion.2), channel_id=1, source_target_pairs={{0,24},{4,28},{8,16},{12,20},{16,8},{20,12},{24,0},{28,4},{1,25},{... | collective-permute-start | bytes 98312 | tf_op jit(solution)/shard_map/ppermute | solution.py:20
  65.2 1.3 %constant_dynamic-update-slice_fusion.15 = bf16[64,256]{1,0:T(8,128)(2,1)} fusion(bf16[64,2048]{1,0:T(8,128)(2,1)} %convolution_convert_fusion, s32[]{:T(128)S(6)} %add.528, s32[]{:T(128)S(6)} %select_n.121), kind=kLoop, calls=%fused_computation.54 | loop fusion | bytes 8200
  66.5 1.3 %constant_dynamic-update-slice_fusion.14 = (bf16[64,256]{1,0:T(8,128)(2,1)}, bf16[64,256]{1,0:T(8,128)(2,1)}, bf16[64,256]{1,0:T(8,128)(2,1)}, bf16[64,256]{1,0:T(8,128)(2,1)}) fusion(bf16[64,256]{1,0:T(8,128)(2,1)} %constant_dynamic-update-slice_fusion.15, bf16[64,2048]{1,0:T(8,128)(2,1)} %convolution_convert_fusion, s32[]{:T(128)S(6)} %select_n.121, ...), kind=kLoop, calls=%fused_computation.53 | loop fusion | bytes 32796
  67.8 1.3 %constant_dynamic-update-slice_fusion.13 = (bf16[64,256]{1,0:T(8,128)(2,1)}, bf16[64,256]{1,0:T(8,128)(2,1)}, bf16[64,256]{1,0:T(8,128)(2,1)}, bf16[64,256]{1,0:T(8,128)(2,1)}) fusion(bf16[64,256]{1,0:T(8,128)(2,1)} %get-tuple-element.37, bf16[64,2048]{1,0:T(8,128)(2,1)} %convolution_convert_fusion, s32[]{:T(128)S(6)} %add.529, s32[]{:T(128)S(6)} %select_n.121, ...), kind=kLoop, calls=%fused_computation.52 | loop fusion | bytes 32800
  69.1 1.3 %constant_dynamic-update-slice_fusion.12 = (bf16[64,256]{1,0:T(8,128)(2,1)}, bf16[64,256]{1,0:T(8,128)(2,1)}, bf16[64,256]{1,0:T(8,128)(2,1)}, bf16[64,256]{1,0:T(8,128)(2,1)}) fusion(bf16[64,256]{1,0:T(8,128)(2,1)} %get-tuple-element.33, bf16[64,2048]{1,0:T(8,128)(2,1)} %convolution_convert_fusion, s32[]{:T(128)S(6)} %add.530, s32[]{:T(128)S(6)} %select_n.121, ...), kind=kLoop, calls=%fused_computation.51 | loop fusion | bytes 32800
  70.4 1.3 %constant_dynamic-update-slice_fusion.11 = (bf16[64,256]{1,0:T(8,128)(2,1)}, bf16[64,256]{1,0:T(8,128)(2,1)}, bf16[64,256]{1,0:T(8,128)(2,1)}, bf16[64,256]{1,0:T(8,128)(2,1)}) fusion(bf16[64,256]{1,0:T(8,128)(2,1)} %get-tuple-element.29, bf16[64,2048]{1,0:T(8,128)(2,1)} %convolution_convert_fusion, s32[]{:T(128)S(6)} %add.531, s32[]{:T(128)S(6)} %select_n.121, ...), kind=kLoop, calls=%fused_computation.50 | loop fusion | bytes 32796
  71.7 1.3 %constant_dynamic-update-slice_fusion.10 = (bf16[64,256]{1,0:T(8,128)(2,1)}, bf16[64,256]{1,0:T(8,128)(2,1)}, bf16[64,256]{1,0:T(8,128)(2,1)}, bf16[64,256]{1,0:T(8,128)(2,1)}) fusion(bf16[64,256]{1,0:T(8,128)(2,1)} %get-tuple-element.25, bf16[64,2048]{1,0:T(8,128)(2,1)} %convolution_convert_fusion, s32[]{:T(128)S(6)} %add.532, s32[]{:T(128)S(6)} %select_n.121, ...), kind=kLoop, calls=%fused_computation.49 | loop fusion | bytes 32800
  73.0 1.3 %constant_dynamic-update-slice_fusion.9 = (bf16[64,256]{1,0:T(8,128)(2,1)}, bf16[64,256]{1,0:T(8,128)(2,1)}, bf16[64,256]{1,0:T(8,128)(2,1)}, bf16[64,256]{1,0:T(8,128)(2,1)}) fusion(bf16[64,256]{1,0:T(8,128)(2,1)} %get-tuple-element.21, bf16[64,2048]{1,0:T(8,128)(2,1)} %convolution_convert_fusion, s32[]{:T(128)S(6)} %add.533, s32[]{:T(128)S(6)} %select_n.121, ...), kind=kLoop, calls=%fused_computation.48 | loop fusion | bytes 32796
  74.3 1.3 %constant_dynamic-update-slice_fusion.8 = (bf16[64,256]{1,0:T(8,128)(2,1)}, bf16[64,256]{1,0:T(8,128)(2,1)}, bf16[64,256]{1,0:T(8,128)(2,1)}, bf16[64,256]{1,0:T(8,128)(2,1)}) fusion(bf16[64,256]{1,0:T(8,128)(2,1)} %get-tuple-element.17, bf16[64,2048]{1,0:T(8,128)(2,1)} %convolution_convert_fusion, s32[]{:T(128)S(6)} %add.534, s32[]{:T(128)S(6)} %select_n.121, ...), kind=kLoop, calls=%fused_computation.47 | loop fusion | bytes 32800 | tf_op jit(solution)/shard_map/concatenate | solution.py:159
  75.6 1.3 %constant_dynamic-update-slice_fusion.16 = (bf16[64,256]{1,0:T(8,128)(2,1)}, bf16[64,256]{1,0:T(8,128)(2,1)}, bf16[64,256]{1,0:T(8,128)(2,1)}) fusion(bf16[64,256]{1,0:T(8,128)(2,1)} %get-tuple-element.16, bf16[64,2048]{1,0:T(8,128)(2,1)} %convolution_convert_fusion, s32[]{:T(128)S(6)} %add.532, s32[]{:T(128)S(6)} %select_n.123, ...), kind=kLoop, calls=%fused_computation.55 | loop fusion | bytes 24596 | tf_op jit(solution)/shard_map/concatenate | solution.py:159
  76.9 1.7 %collective-permute-start.12 = (bf16[64,256]{1,0:T(8,128)(2,1)}, bf16[64,256]{1,0:T(8,128)(2,1)S(1)}, u32[]{:S(2)}, u32[]{:S(2)}) collective-permute-start(bf16[64,256]{1,0:T(8,128)(2,1)} %get-tuple-element.49), channel_id=1, source_target_pairs={{0,12},{4,8},{8,4},{12,0},{16,28},{20,24},{24,20},{28,16},{1,13},{... | collective-permute-start | bytes 98312 | tf_op jit(solution)/shard_map/ppermute | solution.py:20
  78.6 1.6 %collective-permute-start.16 = (bf16[64,256]{1,0:T(8,128)(2,1)}, bf16[64,256]{1,0:T(8,128)(2,1)}, u32[]{:S(2)}, u32[]{:S(2)}) collective-permute-start(bf16[64,256]{1,0:T(8,128)(2,1)} %get-tuple-element.50), channel_id=1, source_target_pairs={{0,28},{4,24},{8,20},{12,16},{16,12},{20,8},{24,4},{28,0},{1,29},{... | collective-permute-start | bytes 98312 | tf_op jit(solution)/shard_map/ppermute | solution.py:20
  80.2 1.4 %collective-permute-start.10 = (bf16[64,256]{1,0:T(8,128)(2,1)}, bf16[64,256]{1,0:T(8,128)(2,1)}, u32[]{:S(2)}, u32[]{:S(2)}) collective-permute-start(bf16[64,256]{1,0:T(8,128)(2,1)} %get-tuple-element.13), channel_id=1, source_target_pairs={{0,4},{4,0},{8,12},{12,8},{16,20},{20,16},{24,28},{28,24},{1,5},{5... | collective-permute-start | bytes 98312 | tf_op jit(solution)/shard_map/ppermute | solution.py:20
  83.1 1.3 %collective-permute-done.10 = bf16[64,256]{1,0:T(8,128)(2,1)} collective-permute-done((bf16[64,256]{1,0:T(8,128)(2,1)}, bf16[64,256]{1,0:T(8,128)(2,1)}, u32[]{:S(2)}, u32[]{:S(2)}) %collective-permute-start.10) | collective-permute-done | bytes 32800 | tf_op jit(solution)/shard_map/ppermute | solution.py:20
  84.5 0.9 add_convert_fusion
  85.4 3.0 %collective-permute-start.18 = (bf16[64,256]{1,0:T(8,128)(2,1)S(1)}, bf16[64,256]{1,0:T(8,128)(2,1)S(1)}, u32[]{:S(2)}, u32[]{:S(2)}) collective-permute-start(bf16[64,256]{1,0:T(8,128)(2,1)S(1)} %add_convert_fusion), channel_id=1, source_target_pairs={{0,2},{1,3},{2,0},{3,1},{4,6},{5,7},{6,4},{7,5},{8,10},{9,11},{10,... | collective-permute-start | bytes 98312 | tf_op jit(solution)/shard_map/ppermute | solution.py:20
  88.4 1.4 %collective-permute-start.19 = (bf16[64,256]{1,0:T(8,128)(2,1)S(1)}, bf16[64,256]{1,0:T(8,128)(2,1)S(1)}, u32[]{:S(2)}, u32[]{:S(2)}) collective-permute-start(bf16[64,256]{1,0:T(8,128)(2,1)S(1)} %add_convert_fusion), channel_id=1, source_target_pairs={{0,3},{1,2},{2,1},{3,0},{4,7},{5,6},{6,5},{7,4},{8,11},{9,10},{10,... | collective-permute-start | bytes 98312 | tf_op jit(solution)/shard_map/ppermute | solution.py:20
  89.8 0.9 collective-permute-done.18
  90.7 3.4 %collective-permute-done.19 = bf16[64,256]{1,0:T(8,128)(2,1)S(1)} collective-permute-done((bf16[64,256]{1,0:T(8,128)(2,1)S(1)}, bf16[64,256]{1,0:T(8,128)(2,1)S(1)}, u32[]{:S(2)}, u32[]{:S(2)}) %collective-permute-start.19) | collective-permute-done | bytes 32800 | tf_op jit(solution)/shard_map/ppermute | solution.py:20
  94.1 0.9 multiply_reduce_fusion
  95.8 1.4 %collective-permute-start.20 = (f32[9,8]{1,0:T(8,128)S(1)}, f32[9,8]{1,0:T(8,128)}, u32[]{:S(2)}, u32[]{:S(2)}) collective-permute-start(f32[9,8]{1,0:T(8,128)S(1)} %pad_maximum_fusion.4), channel_id=1, source_target_pairs={{0,4},{4,0},{8,12},{12,8},{16,20},{20,16},{24,28},{28,24},{1,5},{5... | collective-permute-start | bytes 872 | tf_op jit(solution)/shard_map/ppermute | solution.py:20
  97.9 1.4 %collective-permute-start.22 = (f32[9,8]{1,0:T(8,128)S(1)}, f32[9,8]{1,0:T(8,128)S(1)}, u32[]{:S(2)}, u32[]{:S(2)}) collective-permute-start(f32[9,8]{1,0:T(8,128)S(1)} %pad_maximum_fusion.4), channel_id=1, source_target_pairs={{0,12},{4,8},{8,4},{12,0},{16,28},{20,24},{24,20},{28,16},{1,13},{... | collective-permute-start | bytes 872 | tf_op jit(solution)/shard_map/ppermute | solution.py:20
  99.2 1.5 %collective-permute-start.24 = (f32[9,8]{1,0:T(8,128)S(1)}, f32[9,8]{1,0:T(8,128)S(1)}, u32[]{:S(2)}, u32[]{:S(2)}) collective-permute-start(f32[9,8]{1,0:T(8,128)S(1)} %pad_maximum_fusion.4), channel_id=1, source_target_pairs={{0,20},{4,16},{8,28},{12,24},{16,4},{20,0},{24,12},{28,8},{1,21},{... | collective-permute-start | bytes 872 | tf_op jit(solution)/shard_map/ppermute | solution.py:20
  101.1 1.5 %collective-permute-start.26 = (f32[9,8]{1,0:T(8,128)S(1)}, f32[9,8]{1,0:T(8,128)S(1)}, u32[]{:S(2)}, u32[]{:S(2)}) collective-permute-start(f32[9,8]{1,0:T(8,128)S(1)} %pad_maximum_fusion.4), channel_id=1, source_target_pairs={{0,28},{4,24},{8,20},{12,16},{16,12},{20,8},{24,4},{28,0},{1,29},{... | collective-permute-start | bytes 872 | tf_op jit(solution)/shard_map/ppermute | solution.py:20
  102.6 2.7 %fusion.43 = f32[64,6656]{1,0:T(8,128)} fusion(bf16[256,6656]{1,0:T(8,128)(2,1)S(1)} %copy-done, bf16[64,256]{1,0:T(8,128)(2,1)S(1)} %collective-permute-done.19, bf16[64,256]{1,0:T(8,128)(2,1)S(1)} %collective-permute-done.18, bf16[64,256]{1,0:T(8,128)(2,1)S(1)} %collective-permute-done.17, bf16[64,256]{1,0:T(8,128)(2,1)S(1)} %add_convert_fusion, ...), kind=kOutput, calls=%fused_computation.97 | convolution fusion | flops 218267648 | bytes 5275652 | tf_op jit(solution)/shard_map/dot_general | solution.py:178
  105.3 0.8 slice_add_fusion
  107.0 0.9 slice_add_fusion.14
  107.8 0.9 slice_add_fusion.28
  108.7 0.9 slice_add_fusion.42
  109.8 1.6 %fusion.23 = bf16[32,6656]{1,0:T(8,128)(2,1)S(1)} fusion(f32[64,6656]{1,0:T(8,128)} %fusion.43, f32[32]{0:T(128)S(1)} %get-tuple-element.84, f32[32]{0:T(128)S(1)} %get-tuple-element.83), kind=kLoop, calls=%fused_computation.23 | loop fusion | flops 851968 | bytes 2130176 | tf_op jit(solution)/shard_map/convert_element_type | solution.py:182
  111.5 1.4 %collective-permute-start.27 = (bf16[8,3328]{1,0:T(8,128)(2,1)S(1)}, bf16[8,3328]{1,0:T(8,128)(2,1)S(1)}, u32[]{:S(2)}, u32[]{:S(2)}) collective-permute-start(bf16[8,3328]{1,0:T(8,128)(2,1)S(1)} %get-tuple-element.54), channel_id=1, source_target_pairs={{0,4},{4,0},{8,12},{12,8},{16,20},{20,16},{24,28},{28,24},{1,5},{5... | collective-permute-start | bytes 159752 | tf_op jit(solution)/shard_map/ppermute | solution.py:20
  112.9 0.8 collective-permute-start.28
  114.3 1.1 collective-permute-start.32
  115.4 1.6 %collective-permute-start.29 = (bf16[8,3328]{1,0:T(8,128)(2,1)S(1)}, bf16[8,3328]{1,0:T(8,128)(2,1)S(1)}, u32[]{:S(2)}, u32[]{:S(2)}) collective-permute-start(bf16[8,3328]{1,0:T(8,128)(2,1)S(1)} %get-tuple-element.58), channel_id=1, source_target_pairs={{0,12},{4,8},{8,4},{12,0},{16,28},{20,24},{24,20},{28,16},{1,13},{... | collective-permute-start | bytes 159752 | tf_op jit(solution)/shard_map/ppermute | solution.py:20
  117.7 0.9 collective-permute-start.30
  118.6 1.9 %collective-permute-done.29 = bf16[8,3328]{1,0:T(8,128)(2,1)S(1)} collective-permute-done((bf16[8,3328]{1,0:T(8,128)(2,1)S(1)}, bf16[8,3328]{1,0:T(8,128)(2,1)S(1)}, u32[]{:S(2)}, u32[]{:S(2)}) %collective-permute-start.29) | collective-permute-done | bytes 53280 | tf_op jit(solution)/shard_map/ppermute | solution.py:20
  120.5 1.4 %collective-permute-done.33 = bf16[8,3328]{1,0:T(8,128)(2,1)S(1)} collective-permute-done((bf16[8,3328]{1,0:T(8,128)(2,1)S(1)}, bf16[8,3328]{1,0:T(8,128)(2,1)S(1)}, u32[]{:S(2)}, u32[]{:S(2)}) %collective-permute-start.33) | collective-permute-done | bytes 53280 | tf_op jit(solution)/shard_map/ppermute | solution.py:20
  (124 shorter events, 18.1 us)
Async XLA Ops:
  0.0 102.6 %copy-start = (bf16[256,6656]{1,0:T(8,128)(2,1)S(1)}, bf16[256,6656]{1,0:T(8,128)(2,1)}, u32[]{:S(2)}) copy-start(bf16[256,6656]{1,0:T(8,128)(2,1)} %param.22) | copy-start | bytes 10223620
  0.0 7.6 %copy-start.1 = (bf16[1,8,4,2,256,128]{5,4,3,2,1,0:T(8,128)(2,1)S(1)}, bf16[1,8,4,2,256,128]{5,4,3,2,1,0:T(8,128)(2,1)}, u32[]{:S(2)}) copy-start(bf16[1,8,4,2,256,128]{5,4,3,2,1,0:T(8,128)(2,1)} %param.15) | copy-start | bytes 12582916
  2.8 5.4 %copy-start.12 = (bf16[1,8,4,2,4,128]{5,4,3,2,1,0:T(4,128)(2,1)S(1)}, bf16[1,8,4,2,4,128]{5,4,3,2,1,0:T(4,128)(2,1)}, u32[]{:S(2)}) copy-start(bf16[1,8,4,2,4,128]{5,4,3,2,1,0:T(4,128)(2,1)} %param.14) | copy-start | bytes 196612
  2.8 7.0 %copy-start.13 = (s32[1,8]{1,0:T(1,128)S(1)}, s32[1,8]{1,0:T(1,128)}, u32[]{:S(2)}) copy-start(s32[1,8]{1,0:T(1,128)} %param.13) | copy-start | bytes 100
  6.6 21.6 %copy-start.2 = (bf16[1,8,2048]{2,1,0:T(8,128)(2,1)S(1)}, bf16[1,8,2048]{2,1,0:T(8,128)(2,1)}, u32[]{:S(2)}) copy-start(bf16[1,8,2048]{2,1,0:T(8,128)(2,1)} %param.12) | copy-start | bytes 98308
  11.1 11.4 %copy-start.4 = (s32[2,32,8]{1,2,0:T(8,128)S(1)}, s32[2,32,8]{1,2,0:T(8,128)}, u32[]{:S(2)}) copy-start(s32[2,32,8]{1,2,0:T(8,128)} %param.18) | copy-start | bytes 6148
  11.8 10.9 %copy-start.5 = (f32[2,32,8]{1,2,0:T(8,128)S(1)}, f32[2,32,8]{1,2,0:T(8,128)}, u32[]{:S(2)}) copy-start(f32[2,32,8]{1,2,0:T(8,128)} %param.19) | copy-start | bytes 6148
  16.8 10.0 %collective-permute-start = (bf16[8,2048]{1,0:T(8,128)(2,1)S(1)}, bf16[8,2048]{1,0:T(8,128)(2,1)}, u32[]{:S(2)}, u32[]{:S(2)}) collective-permute-start(bf16[8,2048]{1,0:T(8,128)(2,1)S(1)} %fusion.17), channel_id=1, source_target_pairs={{0,1},{1,0},{2,3},{3,2},{4,5},{5,4},{6,7},{7,6},{8,9},{9,8},{10,11... | collective-permute-start | bytes 98312 | tf_op jit(solution)/shard_map/ppermute | solution.py:20
  19.9 7.0 %collective-permute-start.1 = (bf16[8,2048]{1,0:T(8,128)(2,1)S(1)}, bf16[8,2048]{1,0:T(8,128)(2,1)}, u32[]{:S(2)}, u32[]{:S(2)}) collective-permute-start(bf16[8,2048]{1,0:T(8,128)(2,1)S(1)} %fusion.17), channel_id=1, source_target_pairs={{0,2},{1,3},{2,0},{3,1},{4,6},{5,7},{6,4},{7,5},{8,10},{9,11},{10,... | collective-permute-start | bytes 98312 | tf_op jit(solution)/shard_map/ppermute | solution.py:20
  22.5 5.8 %collective-permute-start.2 = (bf16[8,2048]{1,0:T(8,128)(2,1)S(1)}, bf16[8,2048]{1,0:T(8,128)(2,1)}, u32[]{:S(2)}, u32[]{:S(2)}) collective-permute-start(bf16[8,2048]{1,0:T(8,128)(2,1)S(1)} %fusion.17), channel_id=1, source_target_pairs={{0,3},{1,2},{2,1},{3,0},{4,7},{5,6},{6,5},{7,4},{8,11},{9,10},{10,... | collective-permute-start | bytes 98312 | tf_op jit(solution)/shard_map/ppermute | solution.py:20
  29.7 7.2 %collective-permute-start.3 = (bf16[8,2048]{1,0:T(8,128)(2,1)}, bf16[8,2048]{1,0:T(8,128)(2,1)S(1)}, u32[]{:S(2)}, u32[]{:S(2)}) collective-permute-start(bf16[8,2048]{1,0:T(8,128)(2,1)} %get-tuple-element.6), channel_id=1, source_target_pairs={{0,4},{4,0},{8,12},{12,8},{16,20},{20,16},{24,28},{28,24},{1,5},{5... | collective-permute-start | bytes 98312 | tf_op jit(solution)/shard_map/ppermute | solution.py:20
  33.3 5.3 %collective-permute-start.4 = (bf16[8,2048]{1,0:T(8,128)(2,1)}, bf16[8,2048]{1,0:T(8,128)(2,1)S(1)}, u32[]{:S(2)}, u32[]{:S(2)}) collective-permute-start(bf16[8,2048]{1,0:T(8,128)(2,1)} %get-tuple-element.6), channel_id=1, source_target_pairs={{0,8},{4,12},{8,0},{12,4},{16,24},{20,28},{24,16},{28,20},{1,9},{5... | collective-permute-start | bytes 98312 | tf_op jit(solution)/shard_map/ppermute | solution.py:20
  34.9 5.4 %collective-permute-start.5 = (bf16[8,2048]{1,0:T(8,128)(2,1)}, bf16[8,2048]{1,0:T(8,128)(2,1)S(1)}, u32[]{:S(2)}, u32[]{:S(2)}) collective-permute-start(bf16[8,2048]{1,0:T(8,128)(2,1)} %get-tuple-element.6), channel_id=1, source_target_pairs={{0,12},{4,8},{8,4},{12,0},{16,28},{20,24},{24,20},{28,16},{1,13},{... | collective-permute-start | bytes 98312 | tf_op jit(solution)/shard_map/ppermute | solution.py:20
  35.3 5.6 %collective-permute-start.6 = (bf16[8,2048]{1,0:T(8,128)(2,1)}, bf16[8,2048]{1,0:T(8,128)(2,1)S(1)}, u32[]{:S(2)}, u32[]{:S(2)}) collective-permute-start(bf16[8,2048]{1,0:T(8,128)(2,1)} %get-tuple-element.6), channel_id=1, source_target_pairs={{0,16},{4,20},{8,24},{12,28},{16,0},{20,4},{24,8},{28,12},{1,17},{... | collective-permute-start | bytes 98312 | tf_op jit(solution)/shard_map/ppermute | solution.py:20
  35.3 6.2 %collective-permute-start.7 = (bf16[8,2048]{1,0:T(8,128)(2,1)}, bf16[8,2048]{1,0:T(8,128)(2,1)S(1)}, u32[]{:S(2)}, u32[]{:S(2)}) collective-permute-start(bf16[8,2048]{1,0:T(8,128)(2,1)} %get-tuple-element.6), channel_id=1, source_target_pairs={{0,20},{4,16},{8,28},{12,24},{16,4},{20,0},{24,12},{28,8},{1,21},{... | collective-permute-start | bytes 98312 | tf_op jit(solution)/shard_map/ppermute | solution.py:20
  37.0 5.2 %collective-permute-start.8 = (bf16[8,2048]{1,0:T(8,128)(2,1)}, bf16[8,2048]{1,0:T(8,128)(2,1)S(1)}, u32[]{:S(2)}, u32[]{:S(2)}) collective-permute-start(bf16[8,2048]{1,0:T(8,128)(2,1)} %get-tuple-element.6), channel_id=1, source_target_pairs={{0,24},{4,28},{8,16},{12,20},{16,8},{20,12},{24,0},{28,4},{1,25},{... | collective-permute-start | bytes 98312 | tf_op jit(solution)/shard_map/ppermute | solution.py:20
  38.7 4.5 %collective-permute-start.9 = (bf16[8,2048]{1,0:T(8,128)(2,1)}, bf16[8,2048]{1,0:T(8,128)(2,1)S(1)}, u32[]{:S(2)}, u32[]{:S(2)}) collective-permute-start(bf16[8,2048]{1,0:T(8,128)(2,1)} %get-tuple-element.6), channel_id=1, source_target_pairs={{0,28},{4,24},{8,20},{12,16},{16,12},{20,8},{24,4},{28,0},{1,29},{... | collective-permute-start | bytes 98312 | tf_op jit(solution)/shard_map/ppermute | solution.py:20
  61.7 16.9 %collective-permute-start.11 = (bf16[64,256]{1,0:T(8,128)(2,1)S(1)}, bf16[64,256]{1,0:T(8,128)(2,1)S(1)}, u32[]{:S(2)}, u32[]{:S(2)}) collective-permute-start(bf16[64,256]{1,0:T(8,128)(2,1)S(1)} %pad_maximum_fusion), channel_id=1, source_target_pairs={{0,8},{4,12},{8,0},{12,4},{16,24},{20,28},{24,16},{28,20},{1,9},{5... | collective-permute-start | bytes 98312 | tf_op jit(solution)/shard_map/ppermute | solution.py:20
  63.2 17.0 %collective-permute-start.13 = (bf16[64,256]{1,0:T(8,128)(2,1)S(1)}, bf16[64,256]{1,0:T(8,128)(2,1)S(1)}, u32[]{:S(2)}, u32[]{:S(2)}) collective-permute-start(bf16[64,256]{1,0:T(8,128)(2,1)S(1)} %pad_maximum_fusion.1), channel_id=1, source_target_pairs={{0,16},{4,20},{8,24},{12,28},{16,0},{20,4},{24,8},{28,12},{1,17},{... | collective-permute-start | bytes 98312 | tf_op jit(solution)/shard_map/ppermute | solution.py:20
  63.8 17.8 %collective-permute-start.15 = (bf16[64,256]{1,0:T(8,128)(2,1)}, bf16[64,256]{1,0:T(8,128)(2,1)S(1)}, u32[]{:S(2)}, u32[]{:S(2)}) collective-permute-start(bf16[64,256]{1,0:T(8,128)(2,1)} %pad_maximum_fusion.2), channel_id=1, source_target_pairs={{0,24},{4,28},{8,16},{12,20},{16,8},{20,12},{24,0},{28,4},{1,25},{... | collective-permute-start | bytes 98312 | tf_op jit(solution)/shard_map/ppermute | solution.py:20
  76.9 5.3 %collective-permute-start.12 = (bf16[64,256]{1,0:T(8,128)(2,1)}, bf16[64,256]{1,0:T(8,128)(2,1)S(1)}, u32[]{:S(2)}, u32[]{:S(2)}) collective-permute-start(bf16[64,256]{1,0:T(8,128)(2,1)} %get-tuple-element.49), channel_id=1, source_target_pairs={{0,12},{4,8},{8,4},{12,0},{16,28},{20,24},{24,20},{28,16},{1,13},{... | collective-permute-start | bytes 98312 | tf_op jit(solution)/shard_map/ppermute | solution.py:20
  78.6 3.9 %collective-permute-start.14 = (bf16[64,256]{1,0:T(8,128)(2,1)}, bf16[64,256]{1,0:T(8,128)(2,1)}, u32[]{:S(2)}, u32[]{:S(2)}) collective-permute-start(bf16[64,256]{1,0:T(8,128)(2,1)} %get-tuple-element.51), channel_id=1, source_target_pairs={{0,20},{4,16},{8,28},{12,24},{16,4},{20,0},{24,12},{28,8},{1,21},{... | collective-permute-start | bytes 98312 | tf_op jit(solution)/shard_map/ppermute | solution.py:20
  78.6 4.6 %collective-permute-start.16 = (bf16[64,256]{1,0:T(8,128)(2,1)}, bf16[64,256]{1,0:T(8,128)(2,1)}, u32[]{:S(2)}, u32[]{:S(2)}) collective-permute-start(bf16[64,256]{1,0:T(8,128)(2,1)} %get-tuple-element.50), channel_id=1, source_target_pairs={{0,28},{4,24},{8,20},{12,16},{16,12},{20,8},{24,4},{28,0},{1,29},{... | collective-permute-start | bytes 98312 | tf_op jit(solution)/shard_map/ppermute | solution.py:20
  80.2 4.2 %collective-permute-start.10 = (bf16[64,256]{1,0:T(8,128)(2,1)}, bf16[64,256]{1,0:T(8,128)(2,1)}, u32[]{:S(2)}, u32[]{:S(2)}) collective-permute-start(bf16[64,256]{1,0:T(8,128)(2,1)} %get-tuple-element.13), channel_id=1, source_target_pairs={{0,4},{4,0},{8,12},{12,8},{16,20},{20,16},{24,28},{28,24},{1,5},{5... | collective-permute-start | bytes 98312 | tf_op jit(solution)/shard_map/ppermute | solution.py:20
  82.2 1.0 copy-start.3
  85.3 4.5 %collective-permute-start.17 = (bf16[64,256]{1,0:T(8,128)(2,1)S(1)}, bf16[64,256]{1,0:T(8,128)(2,1)S(1)}, u32[]{:S(2)}, u32[]{:S(2)}) collective-permute-start(bf16[64,256]{1,0:T(8,128)(2,1)S(1)} %add_convert_fusion), channel_id=1, source_target_pairs={{0,1},{1,0},{2,3},{3,2},{4,5},{5,4},{6,7},{7,6},{8,9},{9,8},{10,11... | collective-permute-start | bytes 98312 | tf_op jit(solution)/shard_map/ppermute | solution.py:20
  85.4 5.3 %collective-permute-start.18 = (bf16[64,256]{1,0:T(8,128)(2,1)S(1)}, bf16[64,256]{1,0:T(8,128)(2,1)S(1)}, u32[]{:S(2)}, u32[]{:S(2)}) collective-permute-start(bf16[64,256]{1,0:T(8,128)(2,1)S(1)} %add_convert_fusion), channel_id=1, source_target_pairs={{0,2},{1,3},{2,0},{3,1},{4,6},{5,7},{6,4},{7,5},{8,10},{9,11},{10,... | collective-permute-start | bytes 98312 | tf_op jit(solution)/shard_map/ppermute | solution.py:20
  88.4 5.7 %collective-permute-start.19 = (bf16[64,256]{1,0:T(8,128)(2,1)S(1)}, bf16[64,256]{1,0:T(8,128)(2,1)S(1)}, u32[]{:S(2)}, u32[]{:S(2)}) collective-permute-start(bf16[64,256]{1,0:T(8,128)(2,1)S(1)} %add_convert_fusion), channel_id=1, source_target_pairs={{0,3},{1,2},{2,1},{3,0},{4,7},{5,6},{6,5},{7,4},{8,11},{9,10},{10,... | collective-permute-start | bytes 98312 | tf_op jit(solution)/shard_map/ppermute | solution.py:20
  95.8 5.0 %collective-permute-start.20 = (f32[9,8]{1,0:T(8,128)S(1)}, f32[9,8]{1,0:T(8,128)}, u32[]{:S(2)}, u32[]{:S(2)}) collective-permute-start(f32[9,8]{1,0:T(8,128)S(1)} %pad_maximum_fusion.4), channel_id=1, source_target_pairs={{0,4},{4,0},{8,12},{12,8},{16,20},{20,16},{24,28},{28,24},{1,5},{5... | collective-permute-start | bytes 872 | tf_op jit(solution)/shard_map/ppermute | solution.py:20
  97.1 4.0 %collective-permute-start.21 = (f32[9,8]{1,0:T(8,128)S(1)}, f32[9,8]{1,0:T(8,128)S(1)}, u32[]{:S(2)}, u32[]{:S(2)}) collective-permute-start(f32[9,8]{1,0:T(8,128)S(1)} %pad_maximum_fusion.4), channel_id=1, source_target_pairs={{0,8},{4,12},{8,0},{12,4},{16,24},{20,28},{24,16},{28,20},{1,9},{5... | collective-permute-start | bytes 872 | tf_op jit(solution)/shard_map/ppermute | solution.py:20
  97.9 7.4 %collective-permute-start.22 = (f32[9,8]{1,0:T(8,128)S(1)}, f32[9,8]{1,0:T(8,128)S(1)}, u32[]{:S(2)}, u32[]{:S(2)}) collective-permute-start(f32[9,8]{1,0:T(8,128)S(1)} %pad_maximum_fusion.4), channel_id=1, source_target_pairs={{0,12},{4,8},{8,4},{12,0},{16,28},{20,24},{24,20},{28,16},{1,13},{... | collective-permute-start | bytes 872 | tf_op jit(solution)/shard_map/ppermute | solution.py:20
  99.2 6.0 %collective-permute-start.23 = (f32[9,8]{1,0:T(8,128)S(1)}, f32[9,8]{1,0:T(8,128)S(1)}, u32[]{:S(2)}, u32[]{:S(2)}) collective-permute-start(f32[9,8]{1,0:T(8,128)S(1)} %pad_maximum_fusion.4), channel_id=1, source_target_pairs={{0,16},{4,20},{8,24},{12,28},{16,0},{20,4},{24,8},{28,12},{1,17},{... | collective-permute-start | bytes 872 | tf_op jit(solution)/shard_map/ppermute | solution.py:20
  99.2 6.0 %collective-permute-start.24 = (f32[9,8]{1,0:T(8,128)S(1)}, f32[9,8]{1,0:T(8,128)S(1)}, u32[]{:S(2)}, u32[]{:S(2)}) collective-permute-start(f32[9,8]{1,0:T(8,128)S(1)} %pad_maximum_fusion.4), channel_id=1, source_target_pairs={{0,20},{4,16},{8,28},{12,24},{16,4},{20,0},{24,12},{28,8},{1,21},{... | collective-permute-start | bytes 872 | tf_op jit(solution)/shard_map/ppermute | solution.py:20
  100.7 4.6 %collective-permute-start.25 = (f32[9,8]{1,0:T(8,128)S(1)}, f32[9,8]{1,0:T(8,128)S(1)}, u32[]{:S(2)}, u32[]{:S(2)}) collective-permute-start(f32[9,8]{1,0:T(8,128)S(1)} %pad_maximum_fusion.4), channel_id=1, source_target_pairs={{0,24},{4,28},{8,16},{12,20},{16,8},{20,12},{24,0},{28,4},{1,25},{... | collective-permute-start | bytes 872 | tf_op jit(solution)/shard_map/ppermute | solution.py:20
  101.1 5.1 %copy-start.6 = (f32[9,8]{1,0:T(8,128)}, f32[9,8]{1,0:T(8,128)S(1)}, u32[]{:S(2)}) copy-start(f32[9,8]{1,0:T(8,128)S(1)} %collective-permute-done.21) | copy-start | bytes 868
  101.1 4.2 %collective-permute-start.26 = (f32[9,8]{1,0:T(8,128)S(1)}, f32[9,8]{1,0:T(8,128)S(1)}, u32[]{:S(2)}, u32[]{:S(2)}) collective-permute-start(f32[9,8]{1,0:T(8,128)S(1)} %pad_maximum_fusion.4), channel_id=1, source_target_pairs={{0,28},{4,24},{8,20},{12,16},{16,12},{20,8},{24,4},{28,0},{1,29},{... | collective-permute-start | bytes 872 | tf_op jit(solution)/shard_map/ppermute | solution.py:20
  105.2 0.9 copy-start.7
  105.3 0.9 copy-start.8
  105.3 0.9 copy-start.9
  105.3 0.9 copy-start.10
  105.3 0.9 copy-start.11
  111.5 5.6 %collective-permute-start.27 = (bf16[8,3328]{1,0:T(8,128)(2,1)S(1)}, bf16[8,3328]{1,0:T(8,128)(2,1)S(1)}, u32[]{:S(2)}, u32[]{:S(2)}) collective-permute-start(bf16[8,3328]{1,0:T(8,128)(2,1)S(1)} %get-tuple-element.54), channel_id=1, source_target_pairs={{0,4},{4,0},{8,12},{12,8},{16,20},{20,16},{24,28},{28,24},{1,5},{5... | collective-permute-start | bytes 159752 | tf_op jit(solution)/shard_map/ppermute | solution.py:20
  112.9 4.8 %collective-permute-start.28 = (bf16[8,3328]{1,0:T(8,128)(2,1)S(1)}, bf16[8,3328]{1,0:T(8,128)(2,1)S(1)}, u32[]{:S(2)}, u32[]{:S(2)}) collective-permute-start(bf16[8,3328]{1,0:T(8,128)(2,1)S(1)} %get-tuple-element.56), channel_id=1, source_target_pairs={{0,8},{4,12},{8,0},{12,4},{16,24},{20,28},{24,16},{28,20},{1,9},{5... | collective-permute-start | bytes 159752 | tf_op jit(solution)/shard_map/ppermute | solution.py:20
  113.7 4.8 %collective-permute-start.31 = (bf16[8,3328]{1,0:T(8,128)(2,1)S(1)}, bf16[8,3328]{1,0:T(8,128)(2,1)S(1)}, u32[]{:S(2)}, u32[]{:S(2)}) collective-permute-start(bf16[8,3328]{1,0:T(8,128)(2,1)S(1)} %get-tuple-element.55), channel_id=1, source_target_pairs={{0,20},{4,16},{8,28},{12,24},{16,4},{20,0},{24,12},{28,8},{1,21},{... | collective-permute-start | bytes 159752 | tf_op jit(solution)/shard_map/ppermute | solution.py:20
  114.3 4.3 %collective-permute-start.32 = (bf16[8,3328]{1,0:T(8,128)(2,1)S(1)}, bf16[8,3328]{1,0:T(8,128)(2,1)S(1)}, u32[]{:S(2)}, u32[]{:S(2)}) collective-permute-start(bf16[8,3328]{1,0:T(8,128)(2,1)S(1)} %get-tuple-element.57), channel_id=1, source_target_pairs={{0,24},{4,28},{8,16},{12,20},{16,8},{20,12},{24,0},{28,4},{1,25},{... | collective-permute-start | bytes 159752 | tf_op jit(solution)/shard_map/ppermute | solution.py:20
  115.4 5.1 %collective-permute-start.29 = (bf16[8,3328]{1,0:T(8,128)(2,1)S(1)}, bf16[8,3328]{1,0:T(8,128)(2,1)S(1)}, u32[]{:S(2)}, u32[]{:S(2)}) collective-permute-start(bf16[8,3328]{1,0:T(8,128)(2,1)S(1)} %get-tuple-element.58), channel_id=1, source_target_pairs={{0,12},{4,8},{8,4},{12,0},{16,28},{20,24},{24,20},{28,16},{1,13},{... | collective-permute-start | bytes 159752 | tf_op jit(solution)/shard_map/ppermute | solution.py:20
  117.0 4.8 %collective-permute-start.33 = (bf16[8,3328]{1,0:T(8,128)(2,1)S(1)}, bf16[8,3328]{1,0:T(8,128)(2,1)S(1)}, u32[]{:S(2)}, u32[]{:S(2)}) collective-permute-start(bf16[8,3328]{1,0:T(8,128)(2,1)S(1)} %get-tuple-element.59), channel_id=1, source_target_pairs={{0,28},{4,24},{8,20},{12,16},{16,12},{20,8},{24,4},{28,0},{1,29},{... | collective-permute-start | bytes 159752 | tf_op jit(solution)/shard_map/ppermute | solution.py:20
  117.7 4.1 %collective-permute-start.30 = (bf16[8,3328]{1,0:T(8,128)(2,1)S(1)}, bf16[8,3328]{1,0:T(8,128)(2,1)S(1)}, u32[]{:S(2)}, u32[]{:S(2)}) collective-permute-start(bf16[8,3328]{1,0:T(8,128)(2,1)S(1)} %constant_dynamic-slice_fusion.4), channel_id=1, source_target_pairs={{0,16},{4,20},{8,24},{12,28},{16,0},{20,4},{24,8},{28,12},{1,17},{... | collective-permute-start | bytes 159752 | tf_op jit(solution)/shard_map/ppermute | solution.py:20
